TPU v7x, 32 devices: a whole 2x2x4 slice. The times are simulated.
32 devices in a mesh: grp: 1, blk: 32 (over z, y, x, core).
Axes of the slice: x: 2, y: 2, z: 4, core: 2. Of those that a mesh axis runs over, the one named last changes fastest.
Arguments:
- grad_out: bfloat16 [128, 1440, 384], P(('grp', 'blk')), may hold values from -6 to 6
- coef_saved: bfloat16 [2, 256, 513, 384], P(None, ('grp', 'blk')), may hold values from -0.0546875 to 0.0546875
- mixing: bfloat16 [384, 384], replicated, may hold values from -0.3125 to 0.3125
- order_pairs: int32 [256], replicated, may hold values from 0 to 255, each once
Outputs:
- grad_in: bfloat16 [128, 1440, 384], P(('grp', 'blk'))
- weight_grad: float32 [384, 384], P(('grp', 'blk'))
Inputs may be any that keep to these rules, and one draw needn't show every extreme that they name: Each pair appears once; position q holds the orders order_pairs[q] and 511 - order_pairs[q]; the device with index i along blk holds positions i * 8 to (i + 1) * 8 - 1 of coef_saved.
All inputs are finite; a program needn't handle non-finite values.
Results may differ from a plain program's by a relative error of at most 0.008.
Values may be sent and summed in bfloat16 or wider, within the bound.
A program may use at most 128 MiB of HBM per device.

v0:
```python
import math

import jax
import jax.numpy as jnp
from jax import lax
from jax.sharding import PartitionSpec as P


def longitude_table(order_pairs, degrees, points):
    slot_orders = jnp.stack([order_pairs, degrees - 1 - order_pairs], axis=1).reshape(-1)
    products = slot_orders[:, None] * jnp.arange(points, dtype=jnp.int32)[None, :] % points
    angles = 2.0 * math.pi / points * products.astype(jnp.float32)
    norm_factor = 1.0 / math.sqrt(points)
    return jnp.concatenate(
        [jnp.cos(angles) * norm_factor, -jnp.sin(angles) * norm_factor], axis=0
    ).astype(jnp.bfloat16)


def legendre_rows(pair_ids, cycle_total, degrees, unrolled):
    colatitude = math.pi * (jnp.arange(cycle_total, dtype=jnp.float32) + 0.5) / cycle_total
    cosine_rows = jnp.cos(colatitude)[None, :]
    sine_rows = jnp.sin(colatitude)[None, :]
    first_order = pair_ids.astype(jnp.float32)[:, None]
    second_order = degrees - 1.0 - first_order
    boundary = degrees - first_order
    rescale_limit = 4294967296.0
    rescale_factor = 1.0 / 4294967296.0
    rescale_log = 32.0 * math.log(2.0)

    def start_log(order_value):
        return 0.5 * (
            jnp.log((2.0 * order_value + 1.0) / (4.0 * math.pi))
            + lax.lgamma(order_value + 0.5)
            - lax.lgamma(order_value + 1.0)
            - 0.5 * math.log(math.pi)
        ) + order_value * jnp.log(sine_rows)

    first_start = start_log(first_order)
    second_start = start_log(second_order)

    def advance(state_triple, row_index):
        previous, earlier, offset = state_triple
        position = row_index.astype(jnp.float32)
        in_first = position < boundary
        harmonic = jnp.where(in_first, first_order, second_order)
        degree = jnp.where(in_first, first_order + position, second_order + position - boundary)
        degree_below = degree - 1.0
        factor_a = jnp.sqrt(
            jnp.maximum(4.0 * degree * degree - 1.0, 1.0)
            / jnp.maximum(degree * degree - harmonic * harmonic, 1.0)
        )
        factor_b = jnp.sqrt(
            jnp.maximum(degree_below * degree_below - harmonic * harmonic, 0.0)
            / jnp.maximum(4.0 * degree_below * degree_below - 1.0, 1.0)
        )
        recurred = factor_a * (cosine_rows * previous - factor_b * earlier)
        restart = degree == harmonic
        recurred = jnp.where(restart, jnp.ones_like(recurred), recurred)
        offset = jnp.where(restart, jnp.where(in_first, first_start, second_start), offset)
        emitted = recurred * jnp.exp(offset)
        too_big = jnp.abs(recurred) > rescale_limit
        next_prev = jnp.where(too_big, recurred * rescale_factor, recurred)
        next_earlier = jnp.where(too_big, previous * rescale_factor, previous)
        next_offset = jnp.where(too_big, offset + rescale_log, offset)
        return ((next_prev, next_earlier, next_offset), emitted)

    empty_rows = jnp.zeros((pair_ids.shape[0], cycle_total), jnp.float32)
    final_state, row_values = lax.scan(
        advance,
        (empty_rows, empty_rows, empty_rows),
        jnp.arange(degrees + 1, dtype=jnp.int32),
        unroll=unrolled,
    )
    legendre_values = jnp.transpose(row_values, (1, 0, 2))
    table_scale = math.sqrt(2.0 * math.pi * math.pi / cycle_total)
    synth_table = (legendre_values * table_scale).astype(jnp.bfloat16)
    anal_table = (legendre_values * (table_scale * sine_rows)).astype(jnp.bfloat16)
    return (synth_table, anal_table, boundary)


def per_device(grad_out, coef_saved, mixing, order_pairs):
    devices = lax.axis_size("blk")
    own_index = lax.axis_index("blk")
    cycle_count = grad_out.shape[0]
    cycle_total = cycle_count * devices
    points = grad_out.shape[1]
    channels = grad_out.shape[2]
    pair_count = coef_saved.shape[1]
    degrees = coef_saved.shape[2] - 1
    lon_table = longitude_table(order_pairs, degrees, points)
    own_pairs = lax.dynamic_slice_in_dim(order_pairs, own_index * pair_count, pair_count)
    synth_table, anal_table, boundary = legendre_rows(own_pairs, cycle_total, degrees, 32)
    in_first = (jnp.arange(degrees + 1, dtype=jnp.float32)[None, :] < boundary)[None, :, :, None]
    spectral = jnp.einsum(
        "sn,jnc->jsc", lon_table, grad_out, preferred_element_type=jnp.float32
    ).astype(jnp.bfloat16)
    spectral = spectral.reshape(cycle_count, 2, degrees, channels)
    received = lax.all_to_all(spectral, "blk", split_axis=2, concat_axis=0, tiled=True)
    item_width = received.shape[3]
    grouped = received.reshape(cycle_total, 2, pair_count, 2, item_width)
    both_parts = jnp.einsum(
        "qkj,jrqtc->trqkc", synth_table, grouped, preferred_element_type=jnp.float32
    )
    coef_grad = jnp.where(in_first, both_parts[0], both_parts[1]).astype(jnp.bfloat16)
    block_rows = channels // devices
    local_total = jnp.einsum(
        "rqkc,rqkd->cd", coef_saved, coef_grad, preferred_element_type=jnp.float32
    )
    summed = lax.psum(local_total, "blk")
    weight_grad = lax.dynamic_slice_in_dim(summed, own_index * block_rows, block_rows, 0)
    mixed_grad = jnp.einsum(
        "rqkd,cd->rqkc", coef_grad, mixing, preferred_element_type=jnp.float32
    ).astype(jnp.bfloat16)
    empty_part = jnp.zeros_like(mixed_grad)
    order_split = jnp.stack(
        [jnp.where(in_first, mixed_grad, empty_part), jnp.where(in_first, empty_part, mixed_grad)]
    )
    cycle_part = jnp.einsum(
        "qkj,trqkc->jrqtc", anal_table, order_split, preferred_element_type=jnp.float32
    ).astype(jnp.bfloat16)
    cycle_part = cycle_part.reshape(cycle_total, 2, 2 * pair_count, channels)
    received = lax.all_to_all(cycle_part, "blk", split_axis=0, concat_axis=2, tiled=True)
    item_width = received.shape[3]
    flat_rows = received.reshape(cycle_count, 2 * degrees, item_width)
    grad_in = jnp.einsum(
        "sn,jsc->jnc", lon_table, flat_rows, preferred_element_type=jnp.float32
    ).astype(jnp.bfloat16)
    return (grad_in, weight_grad)


def solution(mesh):
    return jax.shard_map(
        per_device,
        mesh=mesh,
        in_specs=(P(("grp", "blk"), None, None), P(None, ("grp", "blk"), None, None), P(), P()),
        out_specs=(P(("grp", "blk"), None, None), P(("grp", "blk"), None)),
        check_vma=False,
    )
```

profile of v0, /device:TPU:0, one launch (start us, length us, event | category | flops | bytes accessed | tf_op | source)
XLA Modules:
  0.0 667.6 jit_solution(11118878088924272633)
XLA Ops:
  7.2 0.7 broadcast_subtract_fusion
  8.9 12.8 %multiply_convert_fusion.1 = (bf16[512,1440]{0,1:T(8,128)(2,1)S(1)}, bf16[512,1440]{0,1:T(8,128)(2,1)S(1)}) fusion(s32[512]{0:T(512)S(1)} %mul.5292), kind=kLoop, calls=%fused_computation.893 | loop fusion | flops 10321920 | bytes 2951168 | tf_op jit(solution)/shard_map/convert
  21.7 8.8 %convolution_convert_fusion.2 = bf16[1024,4,384]{2,0,1:T(8,128)(2,1)S(1)} fusion(bf16[4,1440,384]{2,1,0:T(8,128)(2,1)} %param.6, bf16[512,1440]{0,1:T(8,128)(2,1)S(1)} %get-tuple-element.1031, bf16[512,1440]{0,1:T(8,128)(2,1)S(1)} %get-tuple-element.1030), kind=kOutput, calls=%fused_computation.899 | convolution fusion | flops 4537319424 | bytes 10518528 | tf_op jit(solution)/shard_map/sn,jnc->jsc/dot_general | solution.py:94
  30.5 4.9 copy.38
  35.4 7.5 %all-to-all-start = ((bf16[4,2,512,384]{3,1,0,2:T(2,128)(2,1)}), bf16[4,2,512,384]{3,1,0,2:T(2,128)(2,1)S(1)}, u32[]{:S(2)}, u32[]{:S(2)}) async-start(bf16[4,2,512,384]{3,1,0,2:T(2,128)(2,1)} %copy.38), calls=%async_computation | async-start | bytes 6291456 | tf_op jit(solution)/shard_map/all_to_all | solution.py:98
  44.5 411.0 %while.23 = (s32[]{:T(128)}, f32[8,128]{1,0:T(8,128)S(1)}, f32[8,128]{1,0:T(8,128)S(1)}, f32[8,128]{1,0:T(8,128)S(1)}, f32[16,32,8,128]{3,1,0,2:T(8,128)}, /*ind...) while((s32[]{:T(128)}, f32[8,128]{1,0:T(8,128)S(1)}, ...), condition=%wide.region_1.2_spmd.clone.clone.clone.clone, body=%wide.region_0.1_spmd.clone.clone.clone.clone.sunk | while | flops 857634 | bytes 1192384 | solution.py:68
  53.4 0.7 fusion.717
  79.1 0.7 fusion.717
  104.8 0.7 fusion.717
  130.5 0.7 fusion.717
  156.2 0.7 fusion.717
  181.8 0.7 fusion.717
  207.5 0.7 fusion.717
  233.2 0.7 fusion.717
  258.9 0.7 fusion.717
  310.3 0.7 fusion.717
  335.9 0.7 fusion.717
  361.6 0.7 fusion.717
  387.3 0.7 fusion.717
  413.0 0.7 fusion.717
  456.1 4.9 copy.40
  461.0 8.2 %convolution_bitcast_fusion = bf16[2,2,8,513,384]{4,3,0,1,2:T(8,128)(2,1)} fusion(bf16[128,2,8,2,384]{4,1,3,2,0:T(2,128)(2,1)S(1)} %bitcast.1027, f32[1,8,128]{2,0,1:T(1,128)S(1)} %bitcast.1040, f32[512,8,128]{2,0,1:T(8,128)} %bitcast.1038), kind=kOutput, calls=%fused_computation.879 | convolution fusion | flops 1615334400 | bytes 17854464 | tf_op jit(solution)/shard_map/qkj,jrqtc->trqkc/dot_general | solution.py:101
  469.2 10.8 %select_bitcast_fusion.1 = (bf16[1,2,8,513,384]{4,3,1,2,0:T(8,128)(2,1)S(1)}, bf16[1,2,8,513,384]{4,3,1,2,0:T(8,128)(2,1)}) fusion(pred[8,513]{1,0:T(8,128)(4,1)S(1)} %iota_compare_fusion, bf16[384,384]{1,0:T(8,128)(2,1)S(1)} %copy-done, bf16[2,2,8,513,384]{4,3,0,1,2:T(8,128)(2,1)} %convolution_bitcast_fusion), kind=kOutput, calls=%fused_computation.884 | convolution fusion | flops 2433245184 | bytes 25520128 | tf_op jit(solution)/shard_map/rqkd,cd->rqkc/dot_general | solution.py:111
  480.0 7.5 %fusion.529 = bf16[8,2,2,384,128]{4,3,2,1,0:T(8,128)(2,1)S(1)} fusion(f32[1,8,128]{2,0,1:T(1,128)S(1)} %bitcast.1041, f32[512,8,128]{2,0,1:T(8,128)S(1)} %bitcast.1039, f32[128]{0:T(128)S(1)} %broadcast_multiply_fusion, bf16[1,2,8,513,384]{4,3,1,2,0:T(8,128)(2,1)} %get-tuple-element.1029, bf16[1,2,8,513,384]{4,3,1,2,0:T(8,128)(2,1)S(1)} %get-tuple-element.1028), kind=kOutput, calls=%fused_computation.898 | convolution fusion | flops 1623211008 | bytes 17854976 | tf_op jit(solution)/shard_map/qkj,trqkc->jrqtc/dot_general | solution.py:118
  487.5 3.3 copy.47
  490.8 5.7 all-to-all-start.1
  496.5 10.3 %fusion.532 = f32[384,384]{0,1:T(8,128)} fusion(bf16[2,8,513,384]{3,1,2,0:T(8,128)(2,1)} %param.7, bf16[2,2,8,513,384]{4,3,0,1,2:T(8,128)(2,1)} %convolution_bitcast_fusion, pred[8,513]{1,0:T(8,128)(4,1)S(1)} %iota_compare_fusion), kind=kOutput, calls=%fused_computation.903 | convolution fusion | flops 2423789568 | bytes 19505160 | tf_op jit(solution)/shard_map/rqkc,rqkd->cd/dot_general | solution.py:106
  506.8 143.9 %all-reduce.2.cloned.1.call-done = f32[384,384]{0,1:T(8,128)} async-done(((f32[384,384]{0,1:T(8,128)}), f32[384,384]{0,1:T(8,128)}) %all-reduce.2.cloned.1.call-update) | async-done | bytes 589840 | tf_op jit(solution)/shard_map/psum | solution.py:109
  650.8 1.1 constant_dynamic-slice_fusion.1
  651.9 0.7 copy.50
  653.0 1.0 copy-done.4
  654.4 6.3 fusion.522
  (922 shorter events, 81.2 us)
Async XLA Ops:
  7.2 462.1 %copy-start = (bf16[384,384]{1,0:T(8,128)(2,1)S(1)}, bf16[384,384]{1,0:T(8,128)(2,1)}, u32[]{:S(2)}) copy-start(bf16[384,384]{1,0:T(8,128)(2,1)} %param.8) | copy-start | bytes 884740
  21.7 8.8 %copy-start.3 = (bf16[512,1440]{0,1:T(8,128)(2,1)}, bf16[512,1440]{0,1:T(8,128)(2,1)S(1)}, u32[]{:S(2)}) copy-start(bf16[512,1440]{0,1:T(8,128)(2,1)S(1)} %get-tuple-element.1030) | copy-start | bytes 4423684
  21.7 8.8 %copy-start.5 = (bf16[512,1440]{0,1:T(8,128)(2,1)}, bf16[512,1440]{0,1:T(8,128)(2,1)S(1)}, u32[]{:S(2)}) copy-start(bf16[512,1440]{0,1:T(8,128)(2,1)S(1)} %get-tuple-element.1031) | copy-start | bytes 4423684
  35.4 7.6 %copy-start.7 = (s32[256]{0:T(256)S(1)}, s32[256]{0:T(256)}, u32[]{:S(2)}) copy-start(s32[256]{0:T(256)} %param.9) | copy-start | bytes 3076
  35.4 420.3 %all-to-all-start = ((bf16[4,2,512,384]{3,1,0,2:T(2,128)(2,1)}), bf16[4,2,512,384]{3,1,0,2:T(2,128)(2,1)S(1)}, u32[]{:S(2)}, u32[]{:S(2)}) async-start(bf16[4,2,512,384]{3,1,0,2:T(2,128)(2,1)} %copy.38), calls=%async_computation | async-start | bytes 6291456 | tf_op jit(solution)/shard_map/all_to_all | solution.py:98
  469.2 10.8 %copy-start.2 = (f32[16,32,8,128]{3,1,0,2:T(8,128)S(1)}, f32[16,32,8,128]{3,1,0,2:T(8,128)}, u32[]{:S(2)}) copy-start(f32[16,32,8,128]{3,1,0,2:T(8,128)} %get-tuple-element.371) | copy-start | bytes 6291460
  490.8 161.8 %all-to-all-start.1 = ((bf16[128,2,16,384]{3,2,1,0:T(8,128)(2,1)}), bf16[128,2,16,384]{3,2,1,0:T(8,128)(2,1)S(1)}, u32[]{:S(2)}, u32[]{:S(2)}) async-start(bf16[128,2,16,384]{3,2,1,0:T(8,128)(2,1)} %copy.47), calls=%async_computation.1 | async-start | bytes 6291456 | tf_op jit(solution)/shard_map/all_to_all | solution.py:122
  496.4 154.3 %all-reduce.2.cloned.1.call-start = ((), (), s32[]{:S(2)}) async-start(), calls=%async_computation.2 | async-start | bytes 1179648 | tf_op jit(solution)/shard_map/psum | solution.py:109
  652.6 1.4 copy-start.4
  652.6 1.8 copy-start.6
  654.4 6.3 copy-start.1
Sparse Core Ops, SparseCore 0:
  507.0 143.7 all-reduce.1
where the time goes:
time: 672 us; the launch traced here: 668 us
  loops' own time  323 us (48%)
  waiting for transfers between devices  144 us (21%)
  other arithmetic  68.7 us (10%)
  local copies, waits for them, and re-layouts  52 us (8%)
  matrix products  51.9 us (8%)
  between operations  14.9 us (2%)
  starting transfers between devices  13.2 us (2%)
    another operation x1, loops' own time, legendre_rows(): lax.scan(advance, (empty_rows, empty_rows, empty_rows), jnp.arange(degree...  323 us
    psum x1, waiting for transfers between devices, per_device(): summed = lax.psum(local_total, 'blk')  144 us
    while x496, other arithmetic  43.3 us
    slice x34, local copies, waits for them, and re-layouts, legendre_rows(): lax.scan(advance, (empty_rows, empty_rows, empty_rows), jnp.arange(degree...  23.3 us
  transfers between devices with their start and end apart: 3, of which 1 were waited for; matrix products, arithmetic and copies ran while one was open for 15% of the time, Pallas kernels for 0%

commit v1 on v0

v1 whole, which is shorter than its diff:
```python
import functools
import math

import jax
import jax.numpy as jnp
from jax import lax
from jax.experimental import pallas as pl
from jax.experimental.pallas import tpu as pltpu
from jax.sharding import PartitionSpec as P

LANES = 128
VMEM_LIMIT = 48 * 1024 * 1024


def compiler_params(dims=1):
    return pltpu.CompilerParams(
        vmem_limit_bytes=VMEM_LIMIT, dimension_semantics=("arbitrary",) * dims
    )


def cost(flops, moved):
    return pl.CostEstimate(flops=int(flops), bytes_accessed=int(moved), transcendentals=0)


def angle_parts(slot_orders, points):
    devices, slots = slot_orders.shape
    blocks = -(-points // LANES)

    def angles(multiples):
        products = slot_orders[:, :, None] * multiples % points
        return 2.0 * math.pi / points * products.astype(jnp.float32)

    coarse = angles(LANES * jnp.arange(blocks, dtype=jnp.int32))
    fine = angles(jnp.arange(LANES, dtype=jnp.int32))
    norm_factor = 1.0 / math.sqrt(points)
    fine_cos = jnp.cos(fine) * norm_factor
    fine_sin = jnp.sin(fine) * norm_factor
    rows = devices * 2 * slots

    def rows_of(first, second):
        return jnp.stack([first, second], axis=1).reshape(rows, -1)

    coarse_cos, coarse_sin = jnp.cos(coarse), jnp.sin(coarse)
    return (
        rows_of(coarse_cos, coarse_cos),
        rows_of(coarse_sin, coarse_sin),
        rows_of(fine_cos, -fine_sin),
        rows_of(fine_sin, fine_cos),
    )


def spectrum_kernel(points, ca_ref, sa_ref, cb_ref, sb_ref, grid_ref, out_ref, table):
    @pl.when(pl.program_id(0) == 0)
    def _():
        for start in range(0, points, LANES):
            width = min(LANES, points - start)
            at = start // LANES
            part = (
                ca_ref[:, at : at + 1] * cb_ref[:, :width]
                - sa_ref[:, at : at + 1] * sb_ref[:, :width]
            )
            table[:, start : start + width] = part.astype(jnp.bfloat16)

    result = jnp.dot(table[...], grid_ref[0], preferred_element_type=jnp.float32)
    devices, _, rows, channels = out_ref.shape
    out_ref[:, 0] = result.reshape(devices, rows, channels).astype(jnp.bfloat16)


def spectrum(parts, grad_out, devices):
    cycles, points, channels = grad_out.shape
    total = parts[0].shape[0]
    rows = total // devices

    def whole(array):
        return pl.BlockSpec(array.shape, lambda j: (0, 0))

    return pl.pallas_call(
        functools.partial(spectrum_kernel, points),
        grid=(cycles,),
        in_specs=[whole(part) for part in parts]
        + [pl.BlockSpec((1, points, channels), lambda j: (j, 0, 0))],
        out_specs=pl.BlockSpec((devices, 1, rows, channels), lambda j: (0, j, 0, 0)),
        out_shape=jax.ShapeDtypeStruct((devices, cycles, rows, channels), jnp.bfloat16),
        scratch_shapes=[pltpu.VMEM((total, points), jnp.bfloat16)],
        compiler_params=compiler_params(),
        cost_estimate=cost(
            2 * cycles * total * points * channels, 2 * cycles * channels * (points + total)
        ),
    )(*parts, grad_out)


def grid_kernel(points, chunks, *refs):
    tables = refs[: 4 * chunks]
    received = refs[4 * chunks : 5 * chunks]
    out_ref = refs[5 * chunks]
    scratch = refs[5 * chunks + 1 :]

    @pl.when(pl.program_id(0) == 0)
    def _():
        for h in range(chunks):
            ca_ref, sa_ref, cb_ref, sb_ref = tables[4 * h : 4 * h + 4]
            for start in range(0, points, LANES):
                width = min(LANES, points - start)
                at = start // LANES
                part = (
                    ca_ref[at : at + 1, :] * cb_ref[:width, :]
                    - sa_ref[at : at + 1, :] * sb_ref[:width, :]
                )
                scratch[h][start : start + width, :] = part.astype(jnp.bfloat16)

    total = None
    for h in range(chunks):
        devices, _, rows, channels = received[h].shape
        block = received[h][:, 0].reshape(devices * rows, channels)
        term = jnp.dot(scratch[h][...], block, preferred_element_type=jnp.float32)
        total = term if total is None else total + term
    out_ref[0] = total.astype(jnp.bfloat16)


def grid_sum(parts_list, received, points):
    chunks = len(received)
    devices, cycles, rows, channels = received[0].shape
    total = devices * rows
    tables = [part.T for parts in parts_list for part in parts]
    return pl.pallas_call(
        functools.partial(grid_kernel, points, chunks),
        grid=(cycles,),
        in_specs=[pl.BlockSpec(t.shape, lambda j: (0, 0)) for t in tables]
        + [pl.BlockSpec((devices, 1, rows, channels), lambda j: (0, j, 0, 0))] * chunks,
        out_specs=pl.BlockSpec((1, points, channels), lambda j: (j, 0, 0)),
        out_shape=jax.ShapeDtypeStruct((cycles, points, channels), jnp.bfloat16),
        scratch_shapes=[pltpu.VMEM((points, total), jnp.bfloat16)] * chunks,
        compiler_params=compiler_params(),
        cost_estimate=cost(
            2 * cycles * total * points * channels * chunks,
            2 * cycles * channels * (points + total * chunks),
        ),
    )(*tables, *received)


def legendre_kernel(
    pairs, degrees, scale, order_ref, cos_ref, sin_ref, start1_ref, start2_ref,
    synth_ref, anal_ref, values,
):
    group = order_ref.shape[0]
    first_order = order_ref[...]
    second_order = degrees - 1.0 - first_order
    boundary = degrees - first_order
    cosine = cos_ref[...]
    first_start = start1_ref[...]
    second_start = start2_ref[...]
    limit = 4294967296.0
    factor = 1.0 / 4294967296.0
    rescale_log = 32.0 * math.log(2.0)
    rows = degrees + 1

    def advance(row, state):
        previous, earlier, offset = state
        position = jnp.full(first_order.shape, row, jnp.int32).astype(jnp.float32)
        in_first = position < boundary
        harmonic = jnp.where(in_first, first_order, second_order)
        degree = jnp.where(in_first, first_order + position, second_order + position - boundary)
        below = degree - 1.0
        square = harmonic * harmonic
        factor_a = jnp.sqrt(
            jnp.maximum(4.0 * degree * degree - 1.0, 1.0)
            / jnp.maximum(degree * degree - square, 1.0)
        )
        factor_b = jnp.sqrt(
            jnp.maximum(below * below - square, 0.0) / jnp.maximum(4.0 * below * below - 1.0, 1.0)
        )
        restart = degree == harmonic
        recurred = factor_a * (cosine * previous - factor_b * earlier)
        recurred = jnp.where(restart, 1.0, recurred)
        offset = jnp.where(restart, jnp.where(in_first, first_start, second_start), offset)
        values[pl.ds(pl.multiple_of(row * group, group), group), :] = recurred * jnp.exp(offset)
        too_big = jnp.abs(recurred) > limit
        return (
            jnp.where(too_big, recurred * factor, recurred),
            jnp.where(too_big, previous * factor, previous),
            jnp.where(too_big, offset + rescale_log, offset),
        )

    empty = jnp.zeros(first_order.shape, jnp.float32)
    steps = 9
    while rows % steps:
        steps -= 1

    def several(at, state):
        for i in range(steps):
            state = advance(at * steps + i, state)
        return state

    lax.fori_loop(0, rows // steps, several, (empty, empty, empty))

    for q in range(pairs):
        block = values[pl.ds(q, rows, stride=group), :]
        row_index = lax.broadcasted_iota(jnp.int32, block.shape, 0).astype(jnp.float32)
        in_first = row_index < boundary[q : q + 1, :]
        sine = sin_ref[q : q + 1, :]
        for ref, weights in ((synth_ref, scale), (anal_ref, scale * sine)):
            scaled = block * weights
            ref[q, :, :LANES] = jnp.where(in_first, scaled, 0.0).astype(jnp.bfloat16)
            ref[q, :, LANES:] = jnp.where(in_first, 0.0, scaled).astype(jnp.bfloat16)


def legendre_tables(pair_ids, cycle_total, degrees):
    pairs = pair_ids.shape[0]
    group = -(-pairs // 8) * 8
    padded = jnp.concatenate([pair_ids, jnp.zeros((group - pairs,), pair_ids.dtype)])
    colatitude = math.pi * (jnp.arange(cycle_total, dtype=jnp.float32) + 0.5) / cycle_total
    cosine_rows = jnp.cos(colatitude)[None, :]
    sine_rows = jnp.sin(colatitude)[None, :]
    first_order = padded.astype(jnp.float32)[:, None]
    second_order = degrees - 1.0 - first_order

    def start_log(order_value):
        return 0.5 * (
            jnp.log((2.0 * order_value + 1.0) / (4.0 * math.pi))
            + lax.lgamma(order_value + 0.5)
            - lax.lgamma(order_value + 1.0)
            - 0.5 * math.log(math.pi)
        ) + order_value * jnp.log(sine_rows)

    shape = (group, cycle_total)
    operands = [
        jnp.broadcast_to(value, shape)
        for value in (
            first_order, cosine_rows, sine_rows, start_log(first_order), start_log(second_order),
        )
    ]
    rows = degrees + 1
    table = jax.ShapeDtypeStruct((pairs, rows, 2 * cycle_total), jnp.bfloat16)
    return pl.pallas_call(
        functools.partial(
            legendre_kernel, pairs, degrees, math.sqrt(2.0 * math.pi * math.pi / cycle_total)
        ),
        grid=(cycle_total // LANES,),
        in_specs=[pl.BlockSpec((group, LANES), lambda i: (0, i))] * 5,
        out_specs=[pl.BlockSpec((pairs, rows, 2 * LANES), lambda i: (0, 0, i))] * 2,
        out_shape=[table, table],
        scratch_shapes=[pltpu.VMEM((rows * group, LANES), jnp.float32)],
        compiler_params=compiler_params(),
        cost_estimate=cost(2e10, 8 * pairs * rows * cycle_total),
    )(*operands)


def mix_kernel(synth_ref, anal_ref, grouped_ref, saved_ref, mixing_ref, cycle_ref, weight_ref):
    @pl.when(pl.program_id(0) == 0)
    def _():
        weight_ref[...] = jnp.zeros_like(weight_ref)

    channels = mixing_ref.shape[0]
    contract_first = (((0,), (0,)), ((), ()))
    contract_last = (((1,), (1,)), ((), ()))
    coef = jnp.dot(
        synth_ref[0], grouped_ref[0], preferred_element_type=jnp.float32
    ).astype(jnp.bfloat16)
    for r in range(2):
        part = coef[:, r * channels : (r + 1) * channels]
        weight_ref[...] += lax.dot_general(
            saved_ref[r, 0], part, contract_first, preferred_element_type=jnp.float32
        )
        mixed = lax.dot_general(
            part, mixing_ref[...], contract_last, preferred_element_type=jnp.float32
        ).astype(jnp.bfloat16)
        cycle_ref[0, :, r * channels : (r + 1) * channels] = lax.dot_general(
            anal_ref[0], mixed, contract_first, preferred_element_type=jnp.float32
        ).astype(jnp.bfloat16)


def mix(synth, anal, grouped, saved, mixing, first):
    count, depth, width = grouped.shape
    rows, channels = saved.shape[2:]
    return pl.pallas_call(
        mix_kernel,
        grid=(count,),
        in_specs=[
            pl.BlockSpec((1, rows, depth), lambda q: (q + first, 0, 0)),
            pl.BlockSpec((1, rows, depth), lambda q: (q + first, 0, 0)),
            pl.BlockSpec((1, depth, width), lambda q: (q, 0, 0)),
            pl.BlockSpec((2, 1, rows, channels), lambda q: (0, q + first, 0, 0)),
            pl.BlockSpec((channels, channels), lambda q: (0, 0)),
        ],
        out_specs=[
            pl.BlockSpec((1, depth, width), lambda q: (q, 0, 0)),
            pl.BlockSpec((channels, channels), lambda q: (0, 0)),
        ],
        out_shape=[
            jax.ShapeDtypeStruct((count, depth, width), jnp.bfloat16),
            jax.ShapeDtypeStruct((channels, channels), jnp.float32),
        ],
        compiler_params=compiler_params(),
        cost_estimate=cost(
            4 * count * rows * width * (depth + channels), 4 * count * (depth + rows) * width
        ),
    )(synth, anal, grouped, saved, mixing)


def per_device(grad_out, coef_saved, mixing, order_pairs):
    devices = lax.axis_size("blk")
    own_index = lax.axis_index("blk")
    cycle_count, points, channels = grad_out.shape
    cycle_total = cycle_count * devices
    groups = cycle_total // LANES
    pair_count = coef_saved.shape[1]
    degrees = coef_saved.shape[2] - 1
    chunks = 2 if pair_count % 8 == 0 else 1
    size = pair_count // chunks

    by_owner = order_pairs.reshape(devices, pair_count)
    slot_orders = jnp.stack([by_owner, degrees - 1 - by_owner], axis=2)
    parts_list = []
    for h in range(chunks):
        slots = slot_orders[:, h * size : (h + 1) * size].reshape(devices, 2 * size)
        parts_list.append(angle_parts(slots, points))

    exchange = functools.partial(
        lax.all_to_all, axis_name="blk", split_axis=0, concat_axis=0, tiled=True
    )
    own_pairs = lax.dynamic_slice_in_dim(order_pairs, own_index * pair_count, pair_count)
    spectra = []
    for h in range(chunks):
        spectra.append(spectrum(parts_list[h], grad_out, devices))
        if h + 1 < chunks:
            spectra[h], grad_out = lax.optimization_barrier((spectra[h], grad_out))
    own_pairs, spectra[-1] = lax.optimization_barrier((own_pairs, spectra[-1]))
    received = [exchange(s) for s in spectra]
    synth, anal = legendre_tables(own_pairs, cycle_total, degrees)

    returned, weight = [], None
    for h in range(chunks):
        grouped = received[h].reshape(groups, LANES, 2, size, 2, channels)
        grouped = jnp.transpose(grouped, (3, 0, 4, 1, 2, 5))
        grouped = grouped.reshape(size, 2 * cycle_total, 2 * channels)
        cycle_part, share = mix(synth, anal, grouped, coef_saved, mixing, h * size)
        weight = share if weight is None else weight + share
        cycle_part = cycle_part.reshape(size, groups, 2, LANES, 2, channels)
        cycle_part = jnp.transpose(cycle_part, (1, 3, 4, 0, 2, 5))
        returned.append(exchange(cycle_part.reshape(devices, cycle_count, 4 * size, channels)))
    shares = exchange(weight.reshape(devices, channels // devices, channels))
    weight_grad = jnp.sum(shares, axis=0)
    grad_in = grid_sum(parts_list, returned, points)
    return (grad_in, weight_grad)


def solution(mesh):
    return jax.shard_map(
        per_device,
        mesh=mesh,
        in_specs=(P(("grp", "blk"), None, None), P(None, ("grp", "blk"), None, None), P(), P()),
        out_specs=(P(("grp", "blk"), None, None), P(("grp", "blk"), None)),
        check_vma=False,
    )
```

time: 672 us -> 257 us (0.38)
  loops' own time: 323 us -> 0 us
  other arithmetic: 68.7 us -> 4.9 us
  matrix products: 51.9 us -> 0 us
  Pallas kernels: 0 us -> 51.1 us
  waiting for transfers between devices: 144 us -> 117 us
  between operations: 14.9 us -> 0.94 us
  starting transfers between devices: 13.2 us -> 22.6 us
  local copies, waits for them, and re-layouts: 52 us -> 59.1 us
    another operation x1 -> x0, loops' own time: 323 us -> none  [legendre_rows(): lax.scan(advance, (empty_rows, empty_rows, empty_rows), jnp.arange(degree...]
    psum x1 -> x0, waiting for transfers between devices: 144 us -> none  [per_device(): summed = lax.psum(local_total, 'blk')]
    all_to_all x2 -> x5, waiting for transfers between devices: 0.01 us -> 117 us  [the longest x2 60.8 us: per_device(): exchange(cycle_part.reshape(devices, cycle_count, 4 * size, channels))]
    dot_general x6 -> x0, matrix products: 51.9 us -> none  [the longest x1 10.8 us: per_device(): jnp.einsum('rqkd,cd->rqkc', coef_grad, mixing, preferred_element_type=jnp...]
    pallas_call x0 -> x6, Pallas kernels: none -> 51.1 us  [the longest x2 19.5 us: mix(): pl.pallas_call(mix_kernel, grid=(count,), in_specs=[pl.BlockSpec((1, rows...]
    while x496 -> x0, other arithmetic: 43.3 us -> none
    reshape x3 -> x25, local copies, waits for them, and re-layouts: 8.24 us -> 39.5 us  [the longest x4 10.3 us: per_device(): cycle_part = cycle_part.reshape(size, groups, 2, LANES, 2, channels)]
    slice x34 -> x2, local copies, waits for them, and re-layouts: 23.3 us -> 0.01 us  [per_device(): slots = slot_orders[:, h * size:(h + 1) * size].reshape(devices, 2 * size)]
  transfers between devices with their start and end apart: 3 -> 5, of which waited for: 1 -> 5; matrix products, arithmetic and copies ran while one was open for 15% -> 14% of each run, Pallas kernels for 0% -> 6%
where the time goes in v1:
time: 257 us; the launch traced here: 255 us
  waiting for transfers between devices  117 us (46%)
  local copies, waits for them, and re-layouts  59.1 us (23%)
  Pallas kernels  51.1 us (20%)
  starting transfers between devices  22.6 us (9%)
  other arithmetic  4.9 us (2%)
    all_to_all x2, waiting for transfers between devices, per_device(): exchange(cycle_part.reshape(devices, cycle_count, 4 * size, channels))  60.8 us
    all_to_all x2, waiting for transfers between devices, per_device(): received = [exchange(s) for s in spectra]  42 us
    pallas_call x2, Pallas kernels, mix(): pl.pallas_call(mix_kernel, grid=(count,), in_specs=[pl.BlockSpec((1, rows...  19.5 us
    unnamed x31, local copies, waits for them, and re-layouts  17.5 us
    pallas_call x2, Pallas kernels, spectrum(): pl.pallas_call(functools.partial(spectrum_kernel, points), grid=(cycles,)...  16.3 us
    all_to_all x1, waiting for transfers between devices, per_device(): shares = exchange(weight.reshape(devices, channels // devices, channels))  13.9 us
    all_to_all x2, starting transfers between devices, per_device(): received = [exchange(s) for s in spectra]  11.4 us
    reshape x4, local copies, waits for them, and re-layouts, per_device(): cycle_part = cycle_part.reshape(size, groups, 2, LANES, 2, channels)  10.3 us
  transfers between devices with their start and end apart: 5, of which 5 were waited for; matrix products, arithmetic and copies ran while one was open for 14% of the time, Pallas kernels for 6%

profile of v1, /device:TPU:0, one launch (start us, length us, event | category | flops | bytes accessed | tf_op | source)
XLA Modules:
  0.0 255.3 jit_solution(15652020403432368500)
XLA Ops:
  4.7 8.1 %shard_map.59 = bf16[32,4,16,384]{3,2,1,0:T(8,128)(2,1)} custom-call(f32[512,12]{1,0:T(8,128)S(1)} %copy.54.ca_ref, f32[512,12]{1,0:T(8,128)S(1)} %copy.55.sa_ref, f32[512,128]{1,0:T(8,128)S(1)} %bitcast.44, f32[512,128]{1,0:T(8,128)S(1)} %bitcast.42, bf16[4,1440,384]{2,1,0:T(8,128)(2,1)} %grid_ref.2), custom_call_target="tpu_custom_call" | custom-call | flops 2264924160 | bytes 5996544 | tf_op jit(solution)/shard_map/pallas_call | solution.py:77
  13.6 7.3 %all-to-all-start = ((bf16[32,4,16,384]{3,2,1,0:T(8,128)(2,1)}), bf16[32,4,16,384]{3,2,1,0:T(8,128)(2,1)S(1)}, u32[]{:S(2)}, u32[]{:S(2)}) async-start(bf16[32,4,16,384]{3,2,1,0:T(8,128)(2,1)} %shard_map.59), calls=%async_computation | async-start | bytes 3145728 | tf_op jit(solution)/shard_map/all_to_all | solution.py:328
  23.6 8.2 %shard_map.60 = bf16[32,4,16,384]{3,2,1,0:T(8,128)(2,1)} custom-call(f32[512,12]{1,0:T(8,128)S(1)} %copy.56.ca_ref, f32[512,12]{1,0:T(8,128)S(1)} %copy.57.sa_ref, f32[512,128]{1,0:T(8,128)S(1)} %bitcast.48, f32[512,128]{1,0:T(8,128)S(1)} %bitcast.46, bf16[4,1440,384]{2,1,0:T(8,128)(2,1)} %grid_ref.2), custom_call_target="tpu_custom_call" | custom-call | flops 2264924160 | bytes 5996544 | tf_op jit(solution)/shard_map/pallas_call | solution.py:77
  33.2 25.4 %all-to-all-done = bf16[32,4,16,384]{3,2,1,0:T(8,128)(2,1)S(1)} async-done(((bf16[32,4,16,384]{3,2,1,0:T(8,128)(2,1)}), bf16[32,4,16,384]{3,2,1,0:T(8,128)(2,1)S(1)}, u32[]{:S(2)}, u32[]{:S(2)}) %all-to-all-start) | async-done | bytes 1572896 | tf_op jit(solution)/shard_map/all_to_all | solution.py:328
  58.6 4.1 %all-to-all-start.2 = ((bf16[32,4,16,384]{3,2,1,0:T(8,128)(2,1)}), bf16[32,4,16,384]{3,2,1,0:T(8,128)(2,1)}, u32[]{:S(2)}, u32[]{:S(2)}) async-start(bf16[32,4,16,384]{3,2,1,0:T(8,128)(2,1)} %shard_map.60), calls=%async_computation.2 | async-start | bytes 3145728 | tf_op jit(solution)/shard_map/all_to_all | solution.py:328
  62.7 6.3 %copy.59.saved_ref = bf16[2,8,513,384]{3,2,1,0:T(8,128)(2,1)} copy(bf16[2,8,513,384]{3,1,2,0:T(8,128)(2,1)} %param.5) | data formatting | bytes 12607488 | tf_op args[1]
  69.4 6.3 %shard_map.61 = (bf16[8,513,256]{2,1,0:T(8,128)(2,1)S(1)}, bf16[8,513,256]{2,1,0:T(8,128)(2,1)S(1)}) custom-call(f32[8,128]{1,0:T(8,128)S(1)} %broadcast_in_dim.6.order_ref, f32[8,128]{1,0:T(8,128)S(1)} %broadcast_in_dim.7.cos_ref, f32[8,128]{1,0:T(8,128)S(1)} %broadcast_in_dim.8.sin_ref, f32[8,128]{1,0:T(8,128)S(1)} %get-tuple-element.39.start1_ref, ...), custom_call_target="tpu_custom_call" | custom-call | flops 20000000000 | bytes 4202496 | tf_op jit(solution)/shard_map/pallas_call | solution.py:234
  78.5 1.6 reshape.498
  80.0 2.6 %copy.71 = bf16[1,128,2,4,2,384]{5,2,1,4,3,0:T(2,128)(2,1)S(1)} copy(bf16[1,128,2,4,2,384]{5,4,3,2,1,0:T(2,128)(2,1)} %reshape.498) | data formatting | bytes 3145728 | tf_op jit(solution)/shard_map/reshape | solution.py:333
  83.7 16.6 %all-to-all-done.2 = bf16[32,4,16,384]{3,2,1,0:T(8,128)(2,1)} async-done(((bf16[32,4,16,384]{3,2,1,0:T(8,128)(2,1)}), bf16[32,4,16,384]{3,2,1,0:T(8,128)(2,1)}, u32[]{:S(2)}, u32[]{:S(2)}) %all-to-all-start.2) | async-done | bytes 1572896 | tf_op jit(solution)/shard_map/all_to_all | solution.py:328
  100.3 3.5 %reshape.502 = bf16[1,128,2,4,2,384]{5,4,3,2,1,0:T(2,128)(2,1)S(1)} reshape(bf16[32,4,16,384]{3,2,1,0:T(8,128)(2,1)} %all-to-all-done.2) | data formatting | bytes 3145728 | tf_op jit(solution)/shard_map/reshape | solution.py:333
  103.8 2.4 copy.69
  106.1 3.9 %reshape.503.grouped_ref = bf16[4,256,768]{2,1,0:T(8,128)(2,1)S(1)} reshape(bf16[4,1,2,128,2,384]{5,4,3,2,0,1:T(2,128)(2,1)} %bitcast.59) | data formatting | bytes 3145728 | tf_op jit(solution)/shard_map/reshape | solution.py:335
  111.0 1.6 copy-done.12
  112.6 9.5 %shard_map.63 = (bf16[4,256,768]{2,1,0:T(8,128)(2,1)S(1)}, f32[384,384]{1,0:T(8,128)S(1)}) custom-call(bf16[8,513,256]{2,1,0:T(8,128)(2,1)S(1)} %copy-done.12, bf16[8,513,256]{2,1,0:T(8,128)(2,1)} %copy-done.13, bf16[4,256,768]{2,1,0:T(8,128)(2,1)S(1)} %reshape.503.grouped_ref, bf16[2,8,513,384]{3,2,1,0:T(8,128)(2,1)} %copy.59.saved_ref, ...), custom_call_target="tpu_custom_call" | custom-call | flops 4034396160 | bytes 9449472 | tf_op jit(solution)/shard_map/pallas_call | solution.py:275
  122.2 10.0 %shard_map.62 = (bf16[4,256,768]{2,1,0:T(8,128)(2,1)S(1)}, f32[384,384]{1,0:T(8,128)S(1)}) custom-call(bf16[8,513,256]{2,1,0:T(8,128)(2,1)S(1)} %copy-done.12, bf16[8,513,256]{2,1,0:T(8,128)(2,1)} %copy-done.13, bf16[4,256,768]{2,1,0:T(8,128)(2,1)S(1)} %reshape.499.grouped_ref, bf16[2,8,513,384]{3,2,1,0:T(8,128)(2,1)} %copy.59.saved_ref, ...), custom_call_target="tpu_custom_call" | custom-call | flops 4034396160 | bytes 9449472 | tf_op jit(solution)/shard_map/pallas_call | solution.py:275
  133.1 2.1 reshape.506
  135.2 3.9 %all-to-all-start.4 = ((f32[32,12,384]{2,1,0:T(8,128)}), f32[32,12,384]{2,1,0:T(8,128)}, u32[]{:S(2)}, u32[]{:S(2)}) async-start(f32[32,12,384]{2,1,0:T(8,128)} %reshape.506), calls=%async_computation.4 | async-start | bytes 1572864 | tf_op jit(solution)/shard_map/all_to_all | solution.py:341
  140.4 3.8 %copy.68 = bf16[4,1,2,128,2,384]{5,2,0,4,3,1:T(2,128)(2,1)S(1)} copy(bf16[4,1,2,128,2,384]{5,4,3,2,0,1:T(2,128)(2,1)} %reshape.504) | data formatting | bytes 3145728 | tf_op jit(solution)/shard_map/reshape | solution.py:338
  144.3 1.5 reshape.505
  145.8 13.9 %all-to-all-done.4 = f32[32,12,384]{2,1,0:T(8,128)} async-done(((f32[32,12,384]{2,1,0:T(8,128)}), f32[32,12,384]{2,1,0:T(8,128)}, u32[]{:S(2)}, u32[]{:S(2)}) %all-to-all-start.4) | async-done | bytes 589856 | tf_op jit(solution)/shard_map/all_to_all | solution.py:341
  159.7 3.6 %all-to-all-start.3 = ((bf16[32,4,16,384]{3,2,1,0:T(8,128)(2,1)}), bf16[32,4,16,384]{3,2,1,0:T(8,128)(2,1)S(1)}, u32[]{:S(2)}, u32[]{:S(2)}) async-start(bf16[32,4,16,384]{3,2,1,0:T(8,128)(2,1)} %reshape.505), calls=%async_computation.3 | async-start | bytes 3145728 | tf_op jit(solution)/shard_map/all_to_all | solution.py:340
  164.7 3.8 %copy.70 = bf16[4,1,2,128,2,384]{5,2,0,4,3,1:T(2,128)(2,1)S(1)} copy(bf16[4,1,2,128,2,384]{5,4,3,2,0,1:T(2,128)(2,1)} %reshape.500) | data formatting | bytes 3145728 | tf_op jit(solution)/shard_map/reshape | solution.py:338
  168.5 1.5 reshape.501
  170.0 31.1 %all-to-all-done.3.refs_9_ = bf16[32,4,16,384]{3,2,1,0:T(8,128)(2,1)S(1)} async-done(((bf16[32,4,16,384]{3,2,1,0:T(8,128)(2,1)}), bf16[32,4,16,384]{3,2,1,0:T(8,128)(2,1)S(1)}, u32[]{:S(2)}, u32[]{:S(2)}) %all-to-all-start.3) | async-done | bytes 1572896 | tf_op jit(solution)/shard_map/all_to_all | solution.py:340
  201.1 3.8 %all-to-all-start.1 = ((bf16[32,4,16,384]{3,2,1,0:T(8,128)(2,1)}), bf16[32,4,16,384]{3,2,1,0:T(8,128)(2,1)S(1)}, u32[]{:S(2)}, u32[]{:S(2)}) async-start(bf16[32,4,16,384]{3,2,1,0:T(8,128)(2,1)} %reshape.501), calls=%async_computation.1 | async-start | bytes 3145728 | tf_op jit(solution)/shard_map/all_to_all | solution.py:340
  204.8 1.8 copy.52
  206.6 1.8 copy.53
  208.4 1.8 copy.46
  211.0 1.8 reduce_sum.9
  212.8 29.7 %all-to-all-done.1.refs_8_ = bf16[32,4,16,384]{3,2,1,0:T(8,128)(2,1)S(1)} async-done(((bf16[32,4,16,384]{3,2,1,0:T(8,128)(2,1)}), bf16[32,4,16,384]{3,2,1,0:T(8,128)(2,1)S(1)}, u32[]{:S(2)}, u32[]{:S(2)}) %all-to-all-start.1) | async-done | bytes 1572896 | tf_op jit(solution)/shard_map/all_to_all | solution.py:340
  246.4 8.9 %shard_map.64 = bf16[4,1440,384]{2,1,0:T(8,128)(2,1)} custom-call(f32[12,512]{1,0:T(8,128)S(1)} %bitcast.54, f32[12,512]{1,0:T(8,128)S(1)} %bitcast.55, f32[128,512]{1,0:T(8,128)S(1)} %bitcast.52, f32[128,512]{1,0:T(8,128)S(1)} %bitcast.53, f32[12,512]{1,0:T(8,128)S(1)} %bitcast.56, f32[12,512]{1,0:T(8,128)S(1)} %bitcast.57, f32[128,512]{1,0:T(8,128)S(1)} %bitcast.50, ...), custom_call_target="tpu_custom_call" | custom-call | flops 4529848320 | bytes 7569408 | tf_op jit(solution)/shard_map/pallas_call | solution.py:125
  (73 shorter events, 22.2 us)
Async XLA Ops:
  12.9 0.7 copy-start.2
  13.6 7.4 %copy-start.14 = (s32[256]{0:T(256)S(1)}, s32[256]{0:T(256)}, u32[]{:S(2)}) copy-start(s32[256]{0:T(256)} %param.7) | copy-start | bytes 3076
  13.6 45.0 %all-to-all-start = ((bf16[32,4,16,384]{3,2,1,0:T(8,128)(2,1)}), bf16[32,4,16,384]{3,2,1,0:T(8,128)(2,1)S(1)}, u32[]{:S(2)}, u32[]{:S(2)}) async-start(bf16[32,4,16,384]{3,2,1,0:T(8,128)(2,1)} %shard_map.59), calls=%async_computation | async-start | bytes 3145728 | tf_op jit(solution)/shard_map/all_to_all | solution.py:328
  31.8 0.7 copy-start.3
  32.5 0.7 copy-start.4
  58.6 41.7 %all-to-all-start.2 = ((bf16[32,4,16,384]{3,2,1,0:T(8,128)(2,1)}), bf16[32,4,16,384]{3,2,1,0:T(8,128)(2,1)}, u32[]{:S(2)}, u32[]{:S(2)}) async-start(bf16[32,4,16,384]{3,2,1,0:T(8,128)(2,1)} %shard_map.60), calls=%async_computation.2 | async-start | bytes 3145728 | tf_op jit(solution)/shard_map/all_to_all | solution.py:328
  75.7 1.3 copy-start.11
  77.1 1.4 copy-start.13
  110.1 1.0 copy-start.9
  111.0 1.6 copy-start.12
  112.6 9.5 %copy-start.10 = (bf16[384,384]{1,0:T(8,128)(2,1)S(1)}, bf16[384,384]{1,0:T(8,128)(2,1)}, u32[]{:S(2)}) copy-start(bf16[384,384]{1,0:T(8,128)(2,1)} %mixing_ref.3) | copy-start | bytes 884740
  122.1 10.1 %copy-start = (bf16[4,256,768]{2,1,0:T(8,128)(2,1)}, bf16[4,256,768]{2,1,0:T(8,128)(2,1)S(1)}, u32[]{:S(2)}) copy-start(bf16[4,256,768]{2,1,0:T(8,128)(2,1)S(1)} %get-tuple-element.19) | copy-start | bytes 4718596
  133.1 6.0 %copy-start.1 = (bf16[4,256,768]{2,1,0:T(8,128)(2,1)S(1)}, bf16[4,256,768]{2,1,0:T(8,128)(2,1)}, u32[]{:S(2)}) copy-start(bf16[4,256,768]{2,1,0:T(8,128)(2,1)} %copy-done) | copy-start | bytes 4718596
  135.2 24.5 %all-to-all-start.4 = ((f32[32,12,384]{2,1,0:T(8,128)}), f32[32,12,384]{2,1,0:T(8,128)}, u32[]{:S(2)}, u32[]{:S(2)}) async-start(f32[32,12,384]{2,1,0:T(8,128)} %reshape.506), calls=%async_computation.4 | async-start | bytes 1572864 | tf_op jit(solution)/shard_map/all_to_all | solution.py:341
  159.7 41.4 %all-to-all-start.3 = ((bf16[32,4,16,384]{3,2,1,0:T(8,128)(2,1)}), bf16[32,4,16,384]{3,2,1,0:T(8,128)(2,1)S(1)}, u32[]{:S(2)}, u32[]{:S(2)}) async-start(bf16[32,4,16,384]{3,2,1,0:T(8,128)(2,1)} %reshape.505), calls=%async_computation.3 | async-start | bytes 3145728 | tf_op jit(solution)/shard_map/all_to_all | solution.py:340
  201.1 41.5 %all-to-all-start.1 = ((bf16[32,4,16,384]{3,2,1,0:T(8,128)(2,1)}), bf16[32,4,16,384]{3,2,1,0:T(8,128)(2,1)S(1)}, u32[]{:S(2)}, u32[]{:S(2)}) async-start(bf16[32,4,16,384]{3,2,1,0:T(8,128)(2,1)} %reshape.501), calls=%async_computation.1 | async-start | bytes 3145728 | tf_op jit(solution)/shard_map/all_to_all | solution.py:340
  242.6 1.0 copy-start.5
  243.5 0.9 copy-start.6
  244.5 0.9 copy-start.7
  245.4 0.9 copy-start.8
